TPU v7x, 512 devices: a whole 4x4x16 slice. The times are simulated.
512 devices in a mesh: row: 4 (over z_lo), col: 16 (over z_hi, y), depth: 8 (over x, core).
Axes of the slice: x: 4, y: 4, z: 16 (z_hi: 4, z_lo: 4; z = z_hi * 4 + z_lo), core: 2. Of those that a mesh axis runs over, the one named last changes fastest.
Arguments:
- activations: bfloat16 [8192, 4096], P(('depth', 'row'), 'col'), may hold values from -6 to 6
- gate_grad: bfloat16 [8192, 16384], P(('depth', 'col'), 'row'), may hold values from -6 to 6
- turn_lengths: int32 [64], replicated, may hold values from 1 to 256, 8192 in all
Outputs:
- weight_grad: bfloat16 [4096, 16384], P('col', ('row', 'depth'))
Inputs may be any that keep to these rules, and one draw needn't show every extreme that they name: `turn_lengths`: the 64 lengths sum to 8192; the longest is exactly 256.
All inputs are finite; a program needn't handle non-finite values.
Results may differ from a plain program's by a relative error of at most 0.0043.
Values may be sent and summed in bfloat16 or wider, within the bound.
A program may use at most 64 MiB of HBM per device.

v0:
```python
import jax
import jax.numpy as jnp
from jax import lax
from jax.sharding import PartitionSpec as P


def product_rows(left, right):
    return lax.dot_general(
        left, right, (((0,), (0,)), ((), ())), preferred_element_type=jnp.float32
    )


def local(activations, gate_grad, turn_lengths):
    grad_rows = gate_grad.shape[0]
    group_tokens = grad_rows * lax.axis_size("col")
    first_token = lax.axis_index("depth") * group_tokens + lax.axis_index("col") * grad_rows
    endings = jnp.cumsum(turn_lengths)
    begins = endings - turn_lengths
    token_pos = first_token + jnp.arange(grad_rows, dtype=jnp.int32)
    inside = (token_pos[:, None] >= begins[None, :]) & (token_pos[:, None] < endings[None, :])
    turn_len = jnp.sum(jnp.where(inside, turn_lengths[None, :], 0), axis=1)
    weighted = (gate_grad.astype(jnp.float32) / turn_len.astype(jnp.float32)[:, None]).astype(
        jnp.bfloat16
    )
    gathered = lax.all_gather(activations, "row", axis=0, tiled=True)
    all_grads = lax.all_gather(weighted, "col", axis=0, tiled=True)
    totals = product_rows(gathered, all_grads)
    summed = lax.psum(totals, "depth")
    share = summed.shape[1] // lax.axis_size("depth")
    result = lax.dynamic_slice_in_dim(summed, lax.axis_index("depth") * share, share, 1)
    return result.astype(jnp.bfloat16)


def solution(mesh):
    in_specs = (P(("depth", "row"), "col"), P(("depth", "col"), "row"), P())
    out_specs = P("col", ("row", "depth"))
    return jax.shard_map(local, mesh=mesh, in_specs=in_specs, out_specs=out_specs, check_vma=False)
```

profile of v0, /device:TPU:8, one launch (start us, length us, event | category | flops | bytes accessed | tf_op | source)
XLA Modules:
  0.0 305.5 jit_solution(8354034274886033443)
XLA Ops:
  6.5 0.0 all-gather.2.cloned.1.call-start
  6.5 0.7 copy.8
  7.3 0.1 reduce-window.8
  7.4 0.1 reduce
  7.5 0.7 sub.3
  8.2 0.8 select_reduce_fusion
  9.0 2.1 divide_convert_fusion
  11.1 0.0 all-gather.2.cloned.1.call-update
  11.1 17.1 %all_gather.7 = bf16[1024,256]{1,0:T(8,128)(2,1)S(1)} all-gather(bf16[256,256]{1,0:T(8,128)(2,1)} %param.3), channel_id=1, replica_groups=mesh['row'=4,'col'=16,'depth'=8] {'row'}, dimensions={0}, use_global_device_ids=true | all-gather | bytes 655360 | tf_op jit(solution)/shard_map/all_gather | solution.py:25
  28.2 203.1 %all-gather.2.cloned.1.call-done = bf16[1024,4096]{1,0:T(8,128)(2,1)} async-done(((bf16[64,4096]{1,0:T(8,128)(2,1)}), bf16[1024,4096]{1,0:T(8,128)(2,1)}) %all-gather.2.cloned.1.call-update) | async-done | bytes 8388624 | tf_op jit(solution)/shard_map/all_gather | solution.py:26
  231.3 7.8 %convolution_bitcast_fusion = f32[256,4096]{0,1:T(8,128)} fusion(bf16[1024,4096]{1,0:T(8,128)(2,1)} %all-gather.2.cloned.1.call-done, bf16[1024,256]{1,0:T(8,128)(2,1)S(1)} %all_gather.7), kind=kOutput, calls=%fused_computation | convolution fusion | flops 2147483648 | bytes 13107200 | tf_op jit(solution)/shard_map/dot_general | solution.py:8
  239.1 58.6 %all-reduce.1 = bf16[256,4096]{0,1:T(8,128)(2,1)S(1)} all-reduce(f32[256,4096]{0,1:T(8,128)} %convolution_bitcast_fusion), channel_id=1, replica_groups=mesh['row'=4,'col'=16,'depth'=8] {'depth'}, use_global_device_ids=true, to_apply=%region_2.3 | all-reduce | flops 1048576 | bytes 6291456 | tf_op jit(solution)/shard_map/psum | solution.py:28
  297.8 0.8 copy.9
  (3 shorter events, 0.0 us)
Async XLA Ops:
  6.5 224.8 %all-gather.2.cloned.1.call-start = ((), (), s32[]{:S(2)}) async-start(), calls=%async_computation | async-start | bytes 8912896 | tf_op jit(solution)/shard_map/all_gather | solution.py:26
Sparse Core Ops, SparseCore 0:
  11.2 220.0 all-gather.1
where the time goes:
time: 306 us; the launch traced here: 305 us
  waiting for transfers between devices  203 us (66%)
  blocking collectives  75.7 us (25%)
  between operations  13.4 us (4%)
  matrix products  7.81 us (3%)
  other arithmetic  3.77 us (1%)
    all_gather x1, waiting for transfers between devices, local(): all_grads = lax.all_gather(weighted, 'col', axis=0, tiled=True)  203 us
    psum x1, blocking collectives, local(): summed = lax.psum(totals, 'depth')  58.6 us
    all_gather x1, blocking collectives, local(): gathered = lax.all_gather(activations, 'row', axis=0, tiled=True)  17.1 us
    dot_general x1, matrix products, product_rows(): lax.dot_general(left, right, (((0,), (0,)), ((), ())), preferred_element_...  7.81 us
  transfers between devices with their start and end apart: 1, of which 1 were waited for; matrix products, arithmetic and copies ran while one was open for 0% of the time, Pallas kernels for 0%

commit v1 on v0

--- a/solution.py
+++ b/solution.py
@@ -23,7 +23,9 @@
         jnp.bfloat16
     )
     gathered = lax.all_gather(activations, "row", axis=0, tiled=True)
-    all_grads = lax.all_gather(weighted, "col", axis=0, tiled=True)
+    all_grads = jnp.concatenate(
+        lax.all_to_all(jnp.stack([weighted] * lax.axis_size("col")), "col", 0, 0), axis=0
+    )
     totals = product_rows(gathered, all_grads)
     summed = lax.psum(totals, "depth")
     share = summed.shape[1] // lax.axis_size("depth")

time: 306 us -> 476 us (1.56)
  the two profiles are of different devices: /device:TPU:8 before, /device:TPU:7 now
where the time goes in v1:
time: 476 us; the launch traced here: 475 us
  blocking collectives  441 us (93%)
  starting transfers between devices  17.7 us (4%)
  matrix products  7.81 us (2%)
  local copies, waits for them, and re-layouts  5.88 us (1%)
    all_gather x1, blocking collectives, local(): gathered = lax.all_gather(activations, 'row', axis=0, tiled=True)  383 us
    psum x1, blocking collectives, local(): summed = lax.psum(totals, 'depth')  57.3 us
    all_to_all x1, starting transfers between devices, local(): lax.all_to_all(jnp.stack([weighted] * lax.axis_size('col')), 'col', 0, 0)  17.7 us
  transfers between devices with their start and end apart: 1, of which 0 were waited for; matrix products, arithmetic and copies ran while one was open for 0% of the time, Pallas kernels for 0%

profile of v1, /device:TPU:7, one launch (start us, length us, event | category | flops | bytes accessed | tf_op | source)
XLA Modules:
  0.0 475.2 jit_solution(10597029368198692911)
XLA Ops:
  0.0 0.7 copy.8
  0.7 0.1 reduce-window.8
  0.8 0.1 reduce
  1.0 0.7 sub.3
  1.6 0.8 select_reduce_fusion
  2.5 1.2 divide_convert_fusion
  3.7 4.3 stack.2
  7.9 0.0 copy-start
  7.9 17.7 %all-to-all-start = ((bf16[16,64,4096]{2,1,0:T(8,128)(2,1)}), bf16[16,64,4096]{2,1,0:T(8,128)(2,1)}, u32[]{:S(2)}, u32[]{:S(2)}) async-start(bf16[16,64,4096]{2,1,0:T(8,128)(2,1)} %stack.2), calls=%async_computation | async-start | bytes 16777216 | tf_op jit(solution)/shard_map/all_to_all | solution.py:27
  25.7 0.0 copy-done
  25.7 383.5 %all_gather.3 = bf16[1024,256]{1,0:T(8,128)(2,1)S(1)} all-gather(bf16[256,256]{1,0:T(8,128)(2,1)S(1)} %copy-done), channel_id=1, replica_groups=mesh['row'=4,'col'=16,'depth'=8] {'row'}, dimensions={0}, use_global_device_ids=true | all-gather | bytes 655360 | tf_op jit(solution)/shard_map/all_gather | solution.py:25
  409.2 0.0 all-to-all-done
  409.2 7.8 %convolution_bitcast_fusion = f32[256,4096]{0,1:T(8,128)} fusion(bf16[1024,4096]{1,0:T(8,128)(2,1)} %bitcast.1, bf16[1024,256]{1,0:T(8,128)(2,1)S(1)} %all_gather.3), kind=kOutput, calls=%fused_computation | convolution fusion | flops 2147483648 | bytes 13107200 | tf_op jit(solution)/shard_map/dot_general | solution.py:8
  417.0 57.3 %all-reduce.1 = bf16[256,4096]{0,1:T(8,128)(2,1)S(1)} all-reduce(f32[256,4096]{0,1:T(8,128)} %convolution_bitcast_fusion), channel_id=1, replica_groups=mesh['row'=4,'col'=16,'depth'=8] {'depth'}, use_global_device_ids=true, to_apply=%region_2.3 | all-reduce | flops 1048576 | bytes 6291456 | tf_op jit(solution)/shard_map/psum | solution.py:30
  474.4 0.8 copy.9
  (3 shorter events, 0.0 us)
Async XLA Ops:
  7.9 17.7 %copy-start = (bf16[256,256]{1,0:T(8,128)(2,1)S(1)}, bf16[256,256]{1,0:T(8,128)(2,1)}, u32[]{:S(2)}) copy-start(bf16[256,256]{1,0:T(8,128)(2,1)} %param.3) | copy-start | bytes 393220
  7.9 401.2 %all-to-all-start = ((bf16[16,64,4096]{2,1,0:T(8,128)(2,1)}), bf16[16,64,4096]{2,1,0:T(8,128)(2,1)}, u32[]{:S(2)}, u32[]{:S(2)}) async-start(bf16[16,64,4096]{2,1,0:T(8,128)(2,1)} %stack.2), calls=%async_computation | async-start | bytes 16777216 | tf_op jit(solution)/shard_map/all_to_all | solution.py:27
